TPU v7x, 256 devices: a whole 4x4x8 slice. The times are simulated.
256 devices in a mesh: win: 4 (over y), space: 64 (over z, x, core).
Axes of the slice: x: 4, y: 4, z: 8, core: 2. Of those that a mesh axis runs over, the one named last changes fastest.
Arguments:
- multipliers: float32 [8, 12, 512, 256], P('win', None, 'space'), may hold values from -6 to 6
- increments: float32 [8, 12, 512, 256], P('win', None, 'space'), may hold values from -6 to 6
- background: float32 [8, 12, 512, 256], P('win', None, 'space'), may hold values from -1.8 to 2, as said below
- error_variance: float32 [8, 12, 512, 256], P('win', None, 'space'), may hold values from 0.25 to 4
- report_weights: float32 [8, 4, 16384], P('win', None, 'space'), may hold values from -6 to 6
- report_variance: float32 [8, 4, 16384], P('win', None, 'space'), may hold values from 0.25 to 4
- report_cells: int32 [8, 4, 16384], P('win', None, 'space'), may hold values from 0 to 24319, as said below
- report_offsets: float32 [8, 4, 2, 16384], P('win', None, None, 'space'), may hold values from 0 to 1
- report_counts: int32 [8, 4, 4096], P('win', None, 'space'), may hold values from 1 to 4, as said below
Outputs:
- model_residual: float32 [8, 12, 512, 256], P('win', None, 'space')
- report_residual: float32 [8, 4, 16384], P('win', None, 'space')
- adjoint_image: float32 [8, 12, 512, 256], P('win', None, 'space')
Inputs may be any that keep to these rules, and one draw needn't show every extreme that they name: `report_cells`: entry p of slot s encodes channel c, strip row r below 7 and column q as p = c * 8 * 256 + r * 256 + q, the rows counted inside the slot's home strip. `report_counts`: entry m * 64 + o counts the live slots from home strip m to owner o at that step; they are the first ones of their 4. `background`: channels 3 l and 3 l + 1 hold velocities between -1.8 and 1.8; channel 3 l + 2 holds depths between 0.3 and 2.
All inputs are finite; a program needn't handle non-finite values.
Results may differ from a plain program's by a relative error of at most 0.0003.
Values sent between devices are 32-bit elements; how exact they have to be, the bound alone decides.
No kernel may reach another device: no remote copies, remote signals or barrier semaphores. Data moves between devices by JAX's collectives and lax.ppermute only.
A program may use at most 64 MiB of HBM per device.

v0:
```python
import jax
import jax.numpy as jnp
import numpy as np
from jax import lax
from jax.sharding import PartitionSpec as P

coupling = np.array(
    [[1.0, 0.55, 0.3, 0.15], [0.5, 0.9, 0.45, 0.25], [0.3, 0.4, 0.8, 0.35], [0.1, 0.2, 0.35, 0.7]],
    np.float32,
)
time_step = 0.1
coriolis = 0.3
viscosity = 0.05


def with_halo(block, sides, width):
    for axis, dim in sides:
        count = lax.axis_size(axis)
        forward = [(i, i + 1) for i in range(count - 1)]
        backward = [(target, source) for source, target in forward]
        low = lax.ppermute(
            lax.slice_in_dim(block, block.shape[dim] - width, None, axis=dim), axis, forward
        )
        high = lax.ppermute(lax.slice_in_dim(block, 0, width, axis=dim), axis, backward)
        block = jnp.concatenate([low, block, high], axis=dim)
    return block


def passed_along(value, axis, by):
    count = lax.axis_size(axis)
    pairs = [(i, i + by) for i in range(count) if 0 <= i + by < count]
    return lax.ppermute(value, axis, pairs)


def across(field):
    return 0.5 * (jnp.roll(field, -1, axis=-1) - jnp.roll(field, 1, axis=-1))


def tendency(padded, backdrop):
    centre = padded[:, 1:-1]
    upper_rows = padded[:, 2:]
    lower_rows = padded[:, :-2]
    shaped = (centre.shape[0] // 3, 3, centre.shape[1], centre.shape[2])
    slope_rows = (0.5 * (upper_rows - lower_rows)).reshape(shaped)
    slope_cols = across(centre).reshape(shaped)
    smooth = (
        upper_rows
        + lower_rows
        + jnp.roll(centre, -1, axis=-1)
        + jnp.roll(centre, 1, axis=-1)
        - 4.0 * centre
    ).reshape(shaped)
    fields = centre.reshape(shaped)
    speeds = backdrop.reshape(shaped)
    drift_cols = speeds[:, 0]
    drift_rows = speeds[:, 1]
    column_depth = speeds[:, 2]
    push_cols = jnp.einsum(
        "lm,mrc->lrc", coupling, slope_cols[:, 2], precision=lax.Precision.HIGHEST
    )
    push_rows = jnp.einsum(
        "lm,mrc->lrc", coupling, slope_rows[:, 2], precision=lax.Precision.HIGHEST
    )
    east_rate = (
        -push_cols
        + coriolis * fields[:, 1]
        - drift_cols * slope_cols[:, 0]
        - drift_rows * slope_rows[:, 0]
        + viscosity * smooth[:, 0]
    )
    north_rate = (
        -push_rows
        - coriolis * fields[:, 0]
        - drift_cols * slope_cols[:, 1]
        - drift_rows * slope_rows[:, 1]
        + viscosity * smooth[:, 1]
    )
    height_rate = (
        -column_depth * (slope_cols[:, 0] + slope_rows[:, 1])
        - drift_cols * slope_cols[:, 2]
        - drift_rows * slope_rows[:, 2]
        + viscosity * smooth[:, 2]
    )
    return jnp.stack([east_rate, north_rate, height_rate], axis=1).reshape(centre.shape)


def adjoint_flux(adjoint, backdrop):
    channels = adjoint.shape[0]
    shaped = (channels // 3, 3, adjoint.shape[1], adjoint.shape[2])
    fields = adjoint.reshape(shaped)
    speeds = backdrop.reshape(shaped)
    along_east = fields[:, 0]
    along_north = fields[:, 1]
    along_height = fields[:, 2]
    drift_rows = speeds[:, 1]
    column_depth = speeds[:, 2]
    lifted_north = jnp.einsum("lm,lrc->mrc", coupling, along_north, precision=lax.Precision.HIGHEST)
    east_flux = drift_rows * along_east
    north_flux = column_depth * along_height + drift_rows * along_north
    height_flux = drift_rows * along_height + lifted_north
    return jnp.concatenate([adjoint, east_flux, north_flux, height_flux], axis=0)


def adjoint_rates(padded, adjoint, backdrop):
    channels = adjoint.shape[0]
    levels = channels // 3
    shaped = (levels, 3, adjoint.shape[1], adjoint.shape[2])
    fields = adjoint.reshape(shaped)
    speeds = backdrop.reshape(shaped)
    along_east = fields[:, 0]
    along_north = fields[:, 1]
    along_height = fields[:, 2]
    drift_cols = speeds[:, 0]
    column_depth = speeds[:, 2]
    lifted_east = jnp.einsum("lm,lrc->mrc", coupling, along_east, precision=lax.Precision.HIGHEST)
    upper_rows = padded[:, 2:]
    lower_rows = padded[:, :-2]
    slope_rows = 0.5 * (upper_rows[channels:] - lower_rows[channels:])
    smooth = (
        upper_rows[:channels]
        + lower_rows[:channels]
        + jnp.roll(adjoint, -1, axis=-1)
        + jnp.roll(adjoint, 1, axis=-1)
        - 4.0 * adjoint
    ).reshape(shaped)
    east_rate = (
        across(column_depth * along_height + drift_cols * along_east)
        + slope_rows[:levels]
        - coriolis * along_north
        + viscosity * smooth[:, 0]
    )
    north_rate = (
        slope_rows[levels : 2 * levels]
        + across(drift_cols * along_north)
        + coriolis * along_east
        + viscosity * smooth[:, 1]
    )
    height_rate = (
        across(drift_cols * along_height + lifted_east)
        + slope_rows[2 * levels :]
        + viscosity * smooth[:, 2]
    )
    return jnp.stack([east_rate, north_rate, height_rate], axis=1).reshape(adjoint.shape)


def stencil(points, fractions, offset_rows, strip_rows, total_rows, grid_cols):
    plane_size = strip_rows * grid_cols
    channel = points // plane_size
    within = points % plane_size
    row_place = offset_rows + within // grid_cols
    column = within % grid_cols
    column_next = (column + 1) % grid_cols
    anchor = channel * (total_rows * grid_cols) + row_place * grid_cols
    indices = jnp.stack(
        [
            anchor + column,
            anchor + column_next,
            anchor + grid_cols + column,
            anchor + grid_cols + column_next,
        ]
    )
    share_cols = fractions[0]
    share_rows = fractions[1]
    weights = jnp.stack(
        [
            (1.0 - share_cols) * (1.0 - share_rows),
            share_cols * (1.0 - share_rows),
            (1.0 - share_cols) * share_rows,
            share_cols * share_rows,
        ]
    )
    return (indices, weights)


def sample(current, points, fractions):
    indices, weights = stencil(
        points, fractions, 0, current.shape[1], current.shape[1], current.shape[2]
    )
    return jnp.sum(weights * current.reshape(-1)[indices], axis=0)


def spread(adjoint, points, fractions, loads):
    indices, weights = stencil(
        points, fractions, 0, adjoint.shape[1], adjoint.shape[1], adjoint.shape[2]
    )
    flattened = adjoint.reshape(-1).at[indices.reshape(-1)].add((weights * loads).reshape(-1))
    return flattened.reshape(adjoint.shape)


def forward_window(current, backdrop, points, fractions, masks):
    moments = points.shape[0]
    sampled_list = []
    for moment in range(moments):
        sampled_list.append(sample(current, points[moment], fractions[moment]))
        padded = with_halo(current, (("space", 1),), 1)
        current = current + time_step * tendency(padded, backdrop)
    return (current, jnp.stack(sampled_list) * masks)


def per_device(
    multipliers,
    increments,
    background,
    error_variance,
    report_weights,
    report_variance,
    report_cells,
    report_offsets,
    report_counts,
):
    subwins = increments.shape[0]
    moments = report_cells.shape[1]
    slot_total = report_cells.shape[2]
    capacity = slot_total // lax.axis_size("space")
    live_counts = jnp.repeat(report_counts, capacity, axis=-1)
    slot_place = jnp.arange(slot_total, dtype=jnp.int32) % capacity
    live_mask = (slot_place < live_counts).astype(jnp.float32)
    home_weights = (
        lax.all_to_all(report_weights, "space", split_axis=2, concat_axis=2, tiled=True) * live_mask
    )
    final_states = []
    sampled_list = []
    for window in range(subwins):
        final_state, sampled_here = forward_window(
            increments[window],
            background[window],
            report_cells[window],
            report_offsets[window],
            live_mask[window],
        )
        final_states.append(final_state)
        sampled_list.append(sampled_here)
    sampled = jnp.stack(sampled_list)
    arrived = lax.all_to_all(sampled, "space", split_axis=2, concat_axis=2, tiled=True)
    report_residual = report_variance * report_weights + arrived
    incoming = passed_along(final_states[-1], "win", 1)
    previous = jnp.stack([incoming] + final_states[:-1])
    model_residual = error_variance * multipliers + increments - previous
    following = passed_along(multipliers[0], "win", -1)
    successors = [multipliers[1]] + [following]
    adjoints = []
    for window in range(subwins):
        adjoint = -successors[window]
        for moment in reversed(range(moments)):
            stacked = adjoint_flux(adjoint, background[window])
            padded = with_halo(stacked, (("space", 1),), 1)
            adjoint = adjoint + time_step * adjoint_rates(padded, adjoint, background[window])
            adjoint = spread(
                adjoint,
                report_cells[window, moment],
                report_offsets[window, moment],
                home_weights[window, moment],
            )
        adjoints.append(adjoint)
    images = [multipliers[window] + adjoints[window] for window in range(subwins)]
    return (model_residual, report_residual, jnp.stack(images))


def solution(mesh):
    placed = (
        P("win", None, "space", None),
        P("win", None, "space", None),
        P("win", None, "space", None),
        P("win", None, "space", None),
        P("win", None, "space"),
        P("win", None, "space"),
        P("win", None, "space"),
        P("win", None, None, "space"),
        P("win", None, "space"),
    )
    return jax.shard_map(
        per_device,
        mesh=mesh,
        in_specs=placed,
        out_specs=(
            P("win", None, "space", None),
            P("win", None, "space"),
            P("win", None, "space", None),
        ),
        check_vma=False,
    )
```

profile of v0, /device:TPU:111, one launch (start us, length us, event | category | flops | bytes accessed | tf_op | source)
XLA Modules:
  0.0 370.3 jit_solution(12716924359439389245)
XLA Ops:
  2.2 2.6 collective-permute-start
  4.8 6.3 %collective-permute-start.1 = (f32[12,1,256]{2,1,0:T(1,128)}, f32[12,1,256]{2,1,0:T(1,128)}, u32[]{:S(2)}, u32[]{:S(2)}) collective-permute-start(f32[12,1,256]{2,1,0:T(1,128)} %get-tuple-element.310), channel_id=1, source_target_pairs={{0,1},{1,2},{2,3},{3,4},{4,5},{5,6},{6,7},{7,8},{8,9},{9,10},{10,1... | collective-permute-start | bytes 36872 | tf_op jit(solution)/shard_map/ppermute | solution.py:21
  13.7 7.0 %collective-permute-start.10 = (f32[12,1,256]{2,1,0:T(1,128)}, f32[12,1,256]{2,1,0:T(1,128)}, u32[]{:S(2)}, u32[]{:S(2)}) collective-permute-start(f32[12,1,256]{2,1,0:T(1,128)} %get-tuple-element.348), channel_id=1, source_target_pairs={{0,1},{1,2},{2,3},{3,4},{4,5},{5,6},{6,7},{7,8},{8,9},{9,10},{10,1... | collective-permute-start | bytes 36872 | tf_op jit(solution)/shard_map/ppermute | solution.py:21
  21.5 7.9 %all-to-all-start.1 = ((f32[2,4,256]{1,0,2:T(2,128)}), f32[2,4,256]{1,0,2:T(2,128)S(1)}, u32[]{:S(2)}, u32[]{:S(2)}) async-start(f32[2,4,256]{1,0,2:T(2,128)} %copy.1439), calls=%async_computation.1 | async-start | bytes 524288 | tf_op jit(solution)/shard_map/all_to_all | solution.py:219
  32.3 4.5 %collective-permute-start.18 = (f32[24,1,256]{2,1,0:T(1,128)}, f32[24,1,256]{2,1,0:T(1,128)S(1)}, u32[]{:S(2)}, u32[]{:S(2)}) collective-permute-start(f32[24,1,256]{2,1,0:T(1,128)} %get-tuple-element.166), channel_id=1, source_target_pairs={{0,1},{1,2},{2,3},{3,4},{4,5},{5,6},{6,7},{7,8},{8,9},{9,10},{10,1... | collective-permute-start | bytes 73736 | tf_op jit(solution)/shard_map/ppermute | solution.py:21
  54.9 6.2 %gather_fusion = f32[1024]{0:T(1024)S(1)} fusion(f32[24576]{0:T(1024)S(1)} %bitcast.2386, s32[1024]{0:T(1024)S(1)} %broadcast_clamp_fusion.7), kind=kCustom, calls=%fused_computation | custom fusion | bytes 12288 | tf_op jit(solution)/shard_map/gather | solution.py:179
  61.7 6.2 %gather_fusion.4 = f32[1024]{0:T(1024)S(1)} fusion(f32[24576]{0:T(1024)S(1)} %bitcast.2384, s32[1024]{0:T(1024)S(1)} %broadcast_clamp_fusion.3), kind=kCustom, calls=%fused_computation.4 | custom fusion | bytes 12288 | tf_op jit(solution)/shard_map/gather | solution.py:179
  78.8 7.0 %collective-permute-start.12 = (f32[12,1,256]{2,1,0:T(1,128)}, f32[12,1,256]{2,1,0:T(1,128)}, u32[]{:S(2)}, u32[]{:S(2)}) collective-permute-start(f32[12,1,256]{2,1,0:T(1,128)} %get-tuple-element.340), channel_id=1, source_target_pairs={{0,1},{1,2},{2,3},{3,4},{4,5},{5,6},{6,7},{7,8},{8,9},{9,10},{10,1... | collective-permute-start | bytes 36872 | tf_op jit(solution)/shard_map/ppermute | solution.py:21
  94.0 7.0 %collective-permute-start.3 = (f32[12,1,256]{2,1,0:T(1,128)S(1)}, f32[12,1,256]{2,1,0:T(1,128)S(1)}, u32[]{:S(2)}, u32[]{:S(2)}) collective-permute-start(f32[12,1,256]{2,1,0:T(1,128)S(1)} %copy-done.56), channel_id=1, source_target_pairs={{0,1},{1,2},{2,3},{3,4},{4,5},{5,6},{6,7},{7,8},{8,9},{9,10},{10,1... | collective-permute-start | bytes 36872 | tf_op jit(solution)/shard_map/ppermute | solution.py:21
  109.6 7.0 %collective-permute-start.14 = (f32[12,1,256]{2,1,0:T(1,128)}, f32[12,1,256]{2,1,0:T(1,128)}, u32[]{:S(2)}, u32[]{:S(2)}) collective-permute-start(f32[12,1,256]{2,1,0:T(1,128)} %get-tuple-element.330), channel_id=1, source_target_pairs={{0,1},{1,2},{2,3},{3,4},{4,5},{5,6},{6,7},{7,8},{8,9},{9,10},{10,1... | collective-permute-start | bytes 36872 | tf_op jit(solution)/shard_map/ppermute | solution.py:21
  119.1 7.0 %collective-permute-start.5 = (f32[12,1,256]{2,1,0:T(1,128)}, f32[12,1,256]{2,1,0:T(1,128)S(1)}, u32[]{:S(2)}, u32[]{:S(2)}) collective-permute-start(f32[12,1,256]{2,1,0:T(1,128)} %get-tuple-element.292), channel_id=1, source_target_pairs={{0,1},{1,2},{2,3},{3,4},{4,5},{5,6},{6,7},{7,8},{8,9},{9,10},{10,1... | collective-permute-start | bytes 36872 | tf_op jit(solution)/shard_map/ppermute | solution.py:21
  134.7 6.2 %gather_fusion.3 = f32[1024]{0:T(1024)S(1)} fusion(f32[24576]{0:T(1024)S(1)} %get-tuple-element.67, s32[1024]{0:T(1024)S(1)} %copy-done.55), kind=kCustom, calls=%fused_computation.3 | custom fusion | bytes 12288 | tf_op jit(solution)/shard_map/gather | solution.py:179
  142.8 6.3 %scatter_fusion = f32[24576]{0:T(1024)S(1)} fusion(f32[24576]{0:T(1024)S(1)} %add.5833, s32[1024]{0:T(1024)S(1)} %bitcast.2541, f32[1024]{0:T(1024)S(1)} %bitcast.2545), kind=kCustom, calls=%fused_computation.8 | custom fusion | flops 1024 | bytes 16384 | tf_op jit(solution)/shard_map/scatter-add | solution.py:186
  155.4 7.0 %collective-permute-start.16 = (f32[12,1,256]{2,1,0:T(1,128)}, f32[12,1,256]{2,1,0:T(1,128)}, u32[]{:S(2)}, u32[]{:S(2)}) collective-permute-start(f32[12,1,256]{2,1,0:T(1,128)} %get-tuple-element.320), channel_id=1, source_target_pairs={{0,1},{1,2},{2,3},{3,4},{4,5},{5,6},{6,7},{7,8},{8,9},{9,10},{10,1... | collective-permute-start | bytes 36872 | tf_op jit(solution)/shard_map/ppermute | solution.py:21
  163.3 2.0 collective-permute-start.6
  165.4 7.0 %collective-permute-start.7 = (f32[12,1,256]{2,1,0:T(1,128)}, f32[12,1,256]{2,1,0:T(1,128)}, u32[]{:S(2)}, u32[]{:S(2)}) collective-permute-start(f32[12,1,256]{2,1,0:T(1,128)} %get-tuple-element.282), channel_id=1, source_target_pairs={{0,1},{1,2},{2,3},{3,4},{4,5},{5,6},{6,7},{7,8},{8,9},{9,10},{10,1... | collective-permute-start | bytes 36872 | tf_op jit(solution)/shard_map/ppermute | solution.py:21
  172.4 6.2 %gather_fusion.2 = f32[1024]{0:T(1024)S(1)} fusion(f32[24576]{0:T(1024)S(1)} %get-tuple-element.68, s32[1024]{0:T(1024)S(1)} %copy-done.50), kind=kCustom, calls=%fused_computation.2 | custom fusion | bytes 12288 | tf_op jit(solution)/shard_map/gather | solution.py:179
  179.2 6.1 %gather_fusion.1 = f32[1024]{0:T(1024)S(1)} fusion(f32[24576]{0:T(1024)S(1)} %get-tuple-element.69, s32[1024]{0:T(1024)S(1)} %copy-done.51), kind=kCustom, calls=%fused_computation.1 | custom fusion | bytes 12288 | tf_op jit(solution)/shard_map/gather | solution.py:179
  186.1 6.1 %gather_fusion.7 = f32[1024]{0:T(1024)S(1)} fusion(f32[24576]{0:T(1024)S(1)} %get-tuple-element.98, s32[1024]{0:T(1024)S(1)} %copy-done.52), kind=kCustom, calls=%fused_computation.7 | custom fusion | bytes 12288 | tf_op jit(solution)/shard_map/gather | solution.py:179
  193.0 6.1 %gather_fusion.6 = f32[1024]{0:T(1024)S(1)} fusion(f32[24576]{0:T(1024)S(1)} %get-tuple-element.99, s32[1024]{0:T(1024)S(1)} %copy-done.53), kind=kCustom, calls=%fused_computation.6 | custom fusion | bytes 12288 | tf_op jit(solution)/shard_map/gather | solution.py:179
  200.0 6.2 %gather_fusion.5 = f32[1024]{0:T(1024)S(1)} fusion(f32[24576]{0:T(1024)S(1)} %get-tuple-element.100, s32[1024]{0:T(1024)S(1)} %copy-done.54), kind=kCustom, calls=%fused_computation.5 | custom fusion | bytes 12288 | tf_op jit(solution)/shard_map/gather | solution.py:179
  211.2 7.6 %all-to-all-start = ((f32[2,4,256]{1,0,2:T(2,128)}), f32[2,4,256]{1,0,2:T(2,128)S(1)}, u32[]{:S(2)}, u32[]{:S(2)}) async-start(f32[2,4,256]{1,0,2:T(2,128)} %copy.1446), calls=%async_computation | async-start | bytes 524288 | tf_op jit(solution)/shard_map/all_to_all | solution.py:234
  218.9 4.6 %collective-permute-start.20 = (f32[24,1,256]{2,1,0:T(1,128)S(1)}, f32[24,1,256]{2,1,0:T(1,128)S(1)}, u32[]{:S(2)}, u32[]{:S(2)}) collective-permute-start(f32[24,1,256]{2,1,0:T(1,128)S(1)} %get-tuple-element.158), channel_id=1, source_target_pairs={{0,1},{1,2},{2,3},{3,4},{4,5},{5,6},{6,7},{7,8},{8,9},{9,10},{10,1... | collective-permute-start | bytes 73736 | tf_op jit(solution)/shard_map/ppermute | solution.py:21
  230.1 3.2 collective-permute-start.8
  238.3 6.1 %scatter_fusion.1 = f32[24576]{0:T(1024)S(1)} fusion(f32[24576]{0:T(1024)S(1)} %add.5849, s32[1024]{0:T(1024)S(1)} %bitcast.2537, f32[1024]{0:T(1024)S(1)} %bitcast.2544), kind=kCustom, calls=%fused_computation.9 | custom fusion | flops 1024 | bytes 16384 | tf_op jit(solution)/shard_map/scatter-add | solution.py:186
  245.6 7.2 %collective-permute-start.22 = (f32[24,1,256]{2,1,0:T(1,128)S(1)}, f32[24,1,256]{2,1,0:T(1,128)S(1)}, u32[]{:S(2)}, u32[]{:S(2)}) collective-permute-start(f32[24,1,256]{2,1,0:T(1,128)S(1)} %get-tuple-element.150), channel_id=1, source_target_pairs={{0,1},{1,2},{2,3},{3,4},{4,5},{5,6},{6,7},{7,8},{8,9},{9,10},{10,1... | collective-permute-start | bytes 73736 | tf_op jit(solution)/shard_map/ppermute | solution.py:21
  254.9 6.4 %collective-permute-done.21 = f32[24,1,256]{2,1,0:T(1,128)S(1)} collective-permute-done((f32[24,1,256]{2,1,0:T(1,128)S(1)}, f32[24,1,256]{2,1,0:T(1,128)S(1)}, u32[]{:S(2)}, u32[]{:S(2)}) %collective-permute-start.21) | collective-permute-done | bytes 24608 | tf_op jit(solution)/shard_map/ppermute | solution.py:24
  262.4 6.1 %scatter_fusion.2 = f32[24576]{0:T(1024)S(1)} fusion(f32[24576]{0:T(1024)S(1)} %add.5865, s32[1024]{0:T(1024)S(1)} %bitcast.2536, f32[1024]{0:T(1024)S(1)} %bitcast.2543), kind=kCustom, calls=%fused_computation.10 | custom fusion | flops 1024 | bytes 16384 | tf_op jit(solution)/shard_map/scatter-add | solution.py:186
  269.7 1.9 collective-permute-start.24
  271.6 2.4 collective-permute-start.23
  274.2 5.9 %collective-permute-done.23 = f32[24,1,256]{2,1,0:T(1,128)S(1)} collective-permute-done((f32[24,1,256]{2,1,0:T(1,128)S(1)}, f32[24,1,256]{2,1,0:T(1,128)S(1)}, u32[]{:S(2)}, u32[]{:S(2)}) %collective-permute-start.23) | collective-permute-done | bytes 24608 | tf_op jit(solution)/shard_map/ppermute | solution.py:24
  281.2 6.3 %scatter_fusion.3 = f32[24576]{0:T(1024)S(1)} fusion(f32[24576]{0:T(1024)S(1)} %add.5881, s32[1024]{0:T(1024)S(1)} %bitcast.2535, f32[1024]{0:T(1024)S(1)} %bitcast.2538), kind=kCustom, calls=%fused_computation.11 | custom fusion | flops 1024 | bytes 16384 | tf_op jit(solution)/shard_map/scatter-add | solution.py:186
  287.6 2.2 collective-permute-start.25
  290.6 2.5 collective-permute-done.25
  294.2 3.1 collective-permute-start.27
  299.4 6.4 %collective-permute-done.26 = f32[24,1,256]{2,1,0:T(1,128)S(1)} collective-permute-done((f32[24,1,256]{2,1,0:T(1,128)S(1)}, f32[24,1,256]{2,1,0:T(1,128)S(1)}, u32[]{:S(2)}, u32[]{:S(2)}) %collective-permute-start.26) | collective-permute-done | bytes 24608 | tf_op jit(solution)/shard_map/ppermute | solution.py:24
  307.0 6.1 %scatter_fusion.4 = f32[24576]{0:T(1024)S(1)} fusion(f32[24576]{0:T(1024)S(1)} %bitcast.2383, s32[1024]{0:T(1024)S(1)} %bitcast.2534, f32[1024]{0:T(1024)S(1)} %bitcast.2542), kind=kCustom, calls=%fused_computation.12 | custom fusion | flops 1024 | bytes 16384 | tf_op jit(solution)/shard_map/scatter-add | solution.py:186
  314.2 1.9 collective-permute-start.29
  316.2 2.4 collective-permute-start.28
  318.7 5.9 %collective-permute-done.28 = f32[24,1,256]{2,1,0:T(1,128)S(1)} collective-permute-done((f32[24,1,256]{2,1,0:T(1,128)S(1)}, f32[24,1,256]{2,1,0:T(1,128)S(1)}, u32[]{:S(2)}, u32[]{:S(2)}) %collective-permute-start.28) | collective-permute-done | bytes 24608 | tf_op jit(solution)/shard_map/ppermute | solution.py:24
  325.8 6.1 %scatter_fusion.5 = f32[24576]{0:T(1024)S(1)} fusion(f32[24576]{0:T(1024)S(1)} %add.5914, s32[1024]{0:T(1024)S(1)} %bitcast.2532, f32[1024]{0:T(1024)S(1)} %bitcast.2540), kind=kCustom, calls=%fused_computation.13 | custom fusion | flops 1024 | bytes 16384 | tf_op jit(solution)/shard_map/scatter-add | solution.py:186
  333.1 1.9 collective-permute-start.31
  335.0 2.4 collective-permute-start.30
  337.6 5.9 %collective-permute-done.30 = f32[24,1,256]{2,1,0:T(1,128)S(1)} collective-permute-done((f32[24,1,256]{2,1,0:T(1,128)S(1)}, f32[24,1,256]{2,1,0:T(1,128)S(1)}, u32[]{:S(2)}, u32[]{:S(2)}) %collective-permute-start.30) | collective-permute-done | bytes 24608 | tf_op jit(solution)/shard_map/ppermute | solution.py:24
  344.6 6.1 %scatter_fusion.6 = f32[24576]{0:T(1024)S(1)} fusion(f32[24576]{0:T(1024)S(1)} %add.5930, s32[1024]{0:T(1024)S(1)} %bitcast.2531, f32[1024]{0:T(1024)S(1)} %bitcast.2539), kind=kCustom, calls=%fused_computation.14 | custom fusion | flops 1024 | bytes 16384 | tf_op jit(solution)/shard_map/scatter-add | solution.py:186
  353.8 2.4 collective-permute-start.32
  356.4 5.9 %collective-permute-done.32 = f32[24,1,256]{2,1,0:T(1,128)S(1)} collective-permute-done((f32[24,1,256]{2,1,0:T(1,128)S(1)}, f32[24,1,256]{2,1,0:T(1,128)S(1)}, u32[]{:S(2)}, u32[]{:S(2)}) %collective-permute-start.32) | collective-permute-done | bytes 24608 | tf_op jit(solution)/shard_map/ppermute | solution.py:24
  363.4 6.1 %scatter_fusion.7 = f32[24576]{0:T(1024)S(1)} fusion(f32[24576]{0:T(1024)S(1)} %add.5946, s32[1024]{0:T(1024)S(1)} %bitcast.2530, f32[1024]{0:T(1024)S(1)} %bitcast.2533), kind=kCustom, calls=%fused_computation.15 | custom fusion | flops 1024 | bytes 16384 | tf_op jit(solution)/shard_map/scatter-add | solution.py:186
  (674 shorter events, 113.6 us)
Async XLA Ops:
  2.2 66.6 %collective-permute-start = (f32[12,1,256]{2,1,0:T(1,128)}, f32[12,1,256]{2,1,0:T(1,128)}, u32[]{:S(2)}, u32[]{:S(2)}) collective-permute-start(f32[12,1,256]{2,1,0:T(1,128)} %get-tuple-element.311), channel_id=1, source_target_pairs={{1,0},{2,1},{3,2},{4,3},{5,4},{6,5},{7,6},{8,7},{9,8},{10,9},{11,1... | collective-permute-start | bytes 36872 | tf_op jit(solution)/shard_map/ppermute | solution.py:24
  4.8 65.9 %collective-permute-start.1 = (f32[12,1,256]{2,1,0:T(1,128)}, f32[12,1,256]{2,1,0:T(1,128)}, u32[]{:S(2)}, u32[]{:S(2)}) collective-permute-start(f32[12,1,256]{2,1,0:T(1,128)} %get-tuple-element.310), channel_id=1, source_target_pairs={{0,1},{1,2},{2,3},{3,4},{4,5},{5,6},{6,7},{7,8},{8,9},{9,10},{10,1... | collective-permute-start | bytes 36872 | tf_op jit(solution)/shard_map/ppermute | solution.py:21
  11.1 9.5 %copy-start.57 = (f32[2,4,256]{2,1,0:T(4,128)S(1)}, f32[2,4,256]{2,1,0:T(4,128)}, u32[]{:S(2)}) copy-start(f32[2,4,256]{2,1,0:T(4,128)} %param.45) | copy-start | bytes 24580
  11.8 60.3 %collective-permute-start.9 = (f32[12,1,256]{2,1,0:T(1,128)}, f32[12,1,256]{2,1,0:T(1,128)}, u32[]{:S(2)}, u32[]{:S(2)}) collective-permute-start(f32[12,1,256]{2,1,0:T(1,128)} %get-tuple-element.349), channel_id=1, source_target_pairs={{1,0},{2,1},{3,2},{4,3},{5,4},{6,5},{7,6},{8,7},{9,8},{10,9},{11,1... | collective-permute-start | bytes 36872 | tf_op jit(solution)/shard_map/ppermute | solution.py:24
  13.7 58.4 %collective-permute-start.10 = (f32[12,1,256]{2,1,0:T(1,128)}, f32[12,1,256]{2,1,0:T(1,128)}, u32[]{:S(2)}, u32[]{:S(2)}) collective-permute-start(f32[12,1,256]{2,1,0:T(1,128)} %get-tuple-element.348), channel_id=1, source_target_pairs={{0,1},{1,2},{2,3},{3,4},{4,5},{5,6},{6,7},{7,8},{8,9},{9,10},{10,1... | collective-permute-start | bytes 36872 | tf_op jit(solution)/shard_map/ppermute | solution.py:21
  21.5 66.8 %all-to-all-start.1 = ((f32[2,4,256]{1,0,2:T(2,128)}), f32[2,4,256]{1,0,2:T(2,128)S(1)}, u32[]{:S(2)}, u32[]{:S(2)}) async-start(f32[2,4,256]{1,0,2:T(2,128)} %copy.1439), calls=%async_computation.1 | async-start | bytes 524288 | tf_op jit(solution)/shard_map/all_to_all | solution.py:219
  32.3 86.8 %collective-permute-start.18 = (f32[24,1,256]{2,1,0:T(1,128)}, f32[24,1,256]{2,1,0:T(1,128)S(1)}, u32[]{:S(2)}, u32[]{:S(2)}) collective-permute-start(f32[24,1,256]{2,1,0:T(1,128)} %get-tuple-element.166), channel_id=1, source_target_pairs={{0,1},{1,2},{2,3},{3,4},{4,5},{5,6},{6,7},{7,8},{8,9},{9,10},{10,1... | collective-permute-start | bytes 73736 | tf_op jit(solution)/shard_map/ppermute | solution.py:21
  68.8 57.2 %collective-permute-start.17 = (f32[24,1,256]{2,1,0:T(1,128)}, f32[24,1,256]{2,1,0:T(1,128)}, u32[]{:S(2)}, u32[]{:S(2)}) collective-permute-start(f32[24,1,256]{2,1,0:T(1,128)} %get-tuple-element.165), channel_id=1, source_target_pairs={{1,0},{2,1},{3,2},{4,3},{5,4},{6,5},{7,6},{8,7},{9,8},{10,9},{11,1... | collective-permute-start | bytes 73736 | tf_op jit(solution)/shard_map/ppermute | solution.py:24
  76.8 17.2 %collective-permute-start.11 = (f32[12,1,256]{2,1,0:T(1,128)}, f32[12,1,256]{2,1,0:T(1,128)}, u32[]{:S(2)}, u32[]{:S(2)}) collective-permute-start(f32[12,1,256]{2,1,0:T(1,128)} %get-tuple-element.341), channel_id=1, source_target_pairs={{1,0},{2,1},{3,2},{4,3},{5,4},{6,5},{7,6},{8,7},{9,8},{10,9},{11,1... | collective-permute-start | bytes 36872 | tf_op jit(solution)/shard_map/ppermute | solution.py:24
  78.8 22.2 %collective-permute-start.12 = (f32[12,1,256]{2,1,0:T(1,128)}, f32[12,1,256]{2,1,0:T(1,128)}, u32[]{:S(2)}, u32[]{:S(2)}) collective-permute-start(f32[12,1,256]{2,1,0:T(1,128)} %get-tuple-element.340), channel_id=1, source_target_pairs={{0,1},{1,2},{2,3},{3,4},{4,5},{5,6},{6,7},{7,8},{8,9},{9,10},{10,1... | collective-permute-start | bytes 36872 | tf_op jit(solution)/shard_map/ppermute | solution.py:21
  86.1 17.8 %collective-permute-start.2 = (f32[12,1,256]{2,1,0:T(1,128)}, f32[12,1,256]{2,1,0:T(1,128)}, u32[]{:S(2)}, u32[]{:S(2)}) collective-permute-start(f32[12,1,256]{2,1,0:T(1,128)} %get-tuple-element.303), channel_id=1, source_target_pairs={{1,0},{2,1},{3,2},{4,3},{5,4},{6,5},{7,6},{8,7},{9,8},{10,9},{11,1... | collective-permute-start | bytes 36872 | tf_op jit(solution)/shard_map/ppermute | solution.py:24
  94.0 9.8 %collective-permute-start.3 = (f32[12,1,256]{2,1,0:T(1,128)S(1)}, f32[12,1,256]{2,1,0:T(1,128)S(1)}, u32[]{:S(2)}, u32[]{:S(2)}) collective-permute-start(f32[12,1,256]{2,1,0:T(1,128)S(1)} %copy-done.56), channel_id=1, source_target_pairs={{0,1},{1,2},{2,3},{3,4},{4,5},{5,6},{6,7},{7,8},{8,9},{9,10},{10,1... | collective-permute-start | bytes 36872 | tf_op jit(solution)/shard_map/ppermute | solution.py:21
  107.7 21.2 %collective-permute-start.13 = (f32[12,1,256]{2,1,0:T(1,128)}, f32[12,1,256]{2,1,0:T(1,128)}, u32[]{:S(2)}, u32[]{:S(2)}) collective-permute-start(f32[12,1,256]{2,1,0:T(1,128)} %get-tuple-element.331), channel_id=1, source_target_pairs={{1,0},{2,1},{3,2},{4,3},{5,4},{6,5},{7,6},{8,7},{9,8},{10,9},{11,1... | collective-permute-start | bytes 36872 | tf_op jit(solution)/shard_map/ppermute | solution.py:24
  109.6 19.3 %collective-permute-start.14 = (f32[12,1,256]{2,1,0:T(1,128)}, f32[12,1,256]{2,1,0:T(1,128)}, u32[]{:S(2)}, u32[]{:S(2)}) collective-permute-start(f32[12,1,256]{2,1,0:T(1,128)} %get-tuple-element.330), channel_id=1, source_target_pairs={{0,1},{1,2},{2,3},{3,4},{4,5},{5,6},{6,7},{7,8},{8,9},{9,10},{10,1... | collective-permute-start | bytes 36872 | tf_op jit(solution)/shard_map/ppermute | solution.py:21
  116.9 14.8 %collective-permute-start.4 = (f32[12,1,256]{2,1,0:T(1,128)}, f32[12,1,256]{2,1,0:T(1,128)S(1)}, u32[]{:S(2)}, u32[]{:S(2)}) collective-permute-start(f32[12,1,256]{2,1,0:T(1,128)} %get-tuple-element.293), channel_id=1, source_target_pairs={{1,0},{2,1},{3,2},{4,3},{5,4},{6,5},{7,6},{8,7},{9,8},{10,9},{11,1... | collective-permute-start | bytes 36872 | tf_op jit(solution)/shard_map/ppermute | solution.py:24
  119.1 12.7 %collective-permute-start.5 = (f32[12,1,256]{2,1,0:T(1,128)}, f32[12,1,256]{2,1,0:T(1,128)S(1)}, u32[]{:S(2)}, u32[]{:S(2)}) collective-permute-start(f32[12,1,256]{2,1,0:T(1,128)} %get-tuple-element.292), channel_id=1, source_target_pairs={{0,1},{1,2},{2,3},{3,4},{4,5},{5,6},{6,7},{7,8},{8,9},{9,10},{10,1... | collective-permute-start | bytes 36872 | tf_op jit(solution)/shard_map/ppermute | solution.py:21
  153.5 71.0 %collective-permute-start.15 = (f32[12,1,256]{2,1,0:T(1,128)}, f32[12,1,256]{2,1,0:T(1,128)}, u32[]{:S(2)}, u32[]{:S(2)}) collective-permute-start(f32[12,1,256]{2,1,0:T(1,128)} %get-tuple-element.321), channel_id=1, source_target_pairs={{1,0},{2,1},{3,2},{4,3},{5,4},{6,5},{7,6},{8,7},{9,8},{10,9},{11,1... | collective-permute-start | bytes 36872 | tf_op jit(solution)/shard_map/ppermute | solution.py:24
  155.4 71.1 %collective-permute-start.16 = (f32[12,1,256]{2,1,0:T(1,128)}, f32[12,1,256]{2,1,0:T(1,128)}, u32[]{:S(2)}, u32[]{:S(2)}) collective-permute-start(f32[12,1,256]{2,1,0:T(1,128)} %get-tuple-element.320), channel_id=1, source_target_pairs={{0,1},{1,2},{2,3},{3,4},{4,5},{5,6},{6,7},{7,8},{8,9},{9,10},{10,1... | collective-permute-start | bytes 36872 | tf_op jit(solution)/shard_map/ppermute | solution.py:21
  163.3 9.0 %copy-start.50 = (s32[1024]{0:T(1024)S(1)}, s32[1024]{0:T(1024)}, u32[]{:S(2)}) copy-start(s32[1024]{0:T(1024)} %broadcast_clamp_fusion.5) | copy-start | bytes 12292
  163.3 64.6 %collective-permute-start.6 = (f32[12,1,256]{2,1,0:T(1,128)}, f32[12,1,256]{2,1,0:T(1,128)}, u32[]{:S(2)}, u32[]{:S(2)}) collective-permute-start(f32[12,1,256]{2,1,0:T(1,128)} %get-tuple-element.283), channel_id=1, source_target_pairs={{1,0},{2,1},{3,2},{4,3},{5,4},{6,5},{7,6},{8,7},{9,8},{10,9},{11,1... | collective-permute-start | bytes 36872 | tf_op jit(solution)/shard_map/ppermute | solution.py:24
  165.4 62.5 %collective-permute-start.7 = (f32[12,1,256]{2,1,0:T(1,128)}, f32[12,1,256]{2,1,0:T(1,128)}, u32[]{:S(2)}, u32[]{:S(2)}) collective-permute-start(f32[12,1,256]{2,1,0:T(1,128)} %get-tuple-element.282), channel_id=1, source_target_pairs={{0,1},{1,2},{2,3},{3,4},{4,5},{5,6},{6,7},{7,8},{8,9},{9,10},{10,1... | collective-permute-start | bytes 36872 | tf_op jit(solution)/shard_map/ppermute | solution.py:21
  199.9 8.3 %copy-start.63 = (f32[1,256]{1,0:T(1,128)S(1)}, f32[1,256]{1,0:T(1,128)}, u32[]{:S(2)}) copy-start(f32[1,256]{1,0:T(1,128)} %get-tuple-element.468) | copy-start | bytes 3076
  199.9 8.3 %copy-start.67 = (f32[1,256]{1,0:T(1,128)S(1)}, f32[1,256]{1,0:T(1,128)}, u32[]{:S(2)}) copy-start(f32[1,256]{1,0:T(1,128)} %get-tuple-element.462) | copy-start | bytes 3076
  199.9 8.3 %copy-start.68 = (f32[1,256]{1,0:T(1,128)S(1)}, f32[1,256]{1,0:T(1,128)}, u32[]{:S(2)}) copy-start(f32[1,256]{1,0:T(1,128)} %get-tuple-element.463) | copy-start | bytes 3076
  199.9 8.3 %copy-start.82 = (f32[1,1,256]{2,1,0:T(1,128)S(1)}, f32[1,1,256]{2,1,0:T(1,128)}, u32[]{:S(2)}) copy-start(f32[1,1,256]{2,1,0:T(1,128)} %get-tuple-element.483) | copy-start | bytes 3076
  199.9 9.0 %copy-start.61 = (f32[1,256]{1,0:T(1,128)S(1)}, f32[1,256]{1,0:T(1,128)}, u32[]{:S(2)}) copy-start(f32[1,256]{1,0:T(1,128)} %get-tuple-element.470) | copy-start | bytes 3076
  199.9 9.0 %copy-start.64 = (f32[1,256]{1,0:T(1,128)S(1)}, f32[1,256]{1,0:T(1,128)}, u32[]{:S(2)}) copy-start(f32[1,256]{1,0:T(1,128)} %get-tuple-element.460) | copy-start | bytes 3076
  199.9 9.0 %copy-start.65 = (f32[1,256]{1,0:T(1,128)S(1)}, f32[1,256]{1,0:T(1,128)}, u32[]{:S(2)}) copy-start(f32[1,256]{1,0:T(1,128)} %get-tuple-element.461) | copy-start | bytes 3076
  199.9 9.0 %copy-start.80 = (f32[1,1,256]{2,1,0:T(1,128)S(1)}, f32[1,1,256]{2,1,0:T(1,128)}, u32[]{:S(2)}) copy-start(f32[1,1,256]{2,1,0:T(1,128)} %get-tuple-element.482) | copy-start | bytes 3076
  200.0 9.7 %copy-start.81 = (f32[256]{0:T(256)S(1)}, f32[256]{0:T(256)}, u32[]{:S(2)}) copy-start(f32[256]{0:T(256)} %get-tuple-element.529) | copy-start | bytes 3076
  200.0 9.7 %copy-start.95 = (f32[256]{0:T(256)S(1)}, f32[256]{0:T(256)}, u32[]{:S(2)}) copy-start(f32[256]{0:T(256)} %get-tuple-element.527) | copy-start | bytes 3076
  211.2 22.1 %all-to-all-start = ((f32[2,4,256]{1,0,2:T(2,128)}), f32[2,4,256]{1,0,2:T(2,128)S(1)}, u32[]{:S(2)}, u32[]{:S(2)}) async-start(f32[2,4,256]{1,0,2:T(2,128)} %copy.1446), calls=%async_computation | async-start | bytes 524288 | tf_op jit(solution)/shard_map/all_to_all | solution.py:234
  218.9 16.2 %collective-permute-start.20 = (f32[24,1,256]{2,1,0:T(1,128)S(1)}, f32[24,1,256]{2,1,0:T(1,128)S(1)}, u32[]{:S(2)}, u32[]{:S(2)}) collective-permute-start(f32[24,1,256]{2,1,0:T(1,128)S(1)} %get-tuple-element.158), channel_id=1, source_target_pairs={{0,1},{1,2},{2,3},{3,4},{4,5},{5,6},{6,7},{7,8},{8,9},{9,10},{10,1... | collective-permute-start | bytes 73736 | tf_op jit(solution)/shard_map/ppermute | solution.py:21
  224.6 10.5 %collective-permute-start.19 = (f32[24,1,256]{2,1,0:T(1,128)S(1)}, f32[24,1,256]{2,1,0:T(1,128)S(1)}, u32[]{:S(2)}, u32[]{:S(2)}) collective-permute-start(f32[24,1,256]{2,1,0:T(1,128)S(1)} %get-tuple-element.157), channel_id=1, source_target_pairs={{1,0},{2,1},{3,2},{4,3},{5,4},{6,5},{7,6},{8,7},{9,8},{10,9},{11,1... | collective-permute-start | bytes 73736 | tf_op jit(solution)/shard_map/ppermute | solution.py:24
  230.1 59.8 %collective-permute-start.8 = (f32[12,8,256]{2,1,0:T(8,128)S(1)}, f32[12,8,256]{2,1,0:T(8,128)S(1)}, u32[]{:S(2)}, u32[]{:S(2)}) collective-permute-start(f32[12,8,256]{2,1,0:T(8,128)S(1)} %bitcast_add_fusion.8), channel_id=1, source_target_pairs={{0,64},{64,128},{128,192},{1,65},{65,129},{129,193},{2,66},{66,130... | collective-permute-start | bytes 294920 | tf_op jit(solution)/shard_map/ppermute | solution.py:32
  245.6 9.3 %collective-permute-start.22 = (f32[24,1,256]{2,1,0:T(1,128)S(1)}, f32[24,1,256]{2,1,0:T(1,128)S(1)}, u32[]{:S(2)}, u32[]{:S(2)}) collective-permute-start(f32[24,1,256]{2,1,0:T(1,128)S(1)} %get-tuple-element.150), channel_id=1, source_target_pairs={{0,1},{1,2},{2,3},{3,4},{4,5},{5,6},{6,7},{7,8},{8,9},{9,10},{10,1... | collective-permute-start | bytes 73736 | tf_op jit(solution)/shard_map/ppermute | solution.py:21
  252.8 8.5 %collective-permute-start.21 = (f32[24,1,256]{2,1,0:T(1,128)S(1)}, f32[24,1,256]{2,1,0:T(1,128)S(1)}, u32[]{:S(2)}, u32[]{:S(2)}) collective-permute-start(f32[24,1,256]{2,1,0:T(1,128)S(1)} %get-tuple-element.149), channel_id=1, source_target_pairs={{1,0},{2,1},{3,2},{4,3},{5,4},{6,5},{7,6},{8,7},{9,8},{10,9},{11,1... | collective-permute-start | bytes 73736 | tf_op jit(solution)/shard_map/ppermute | solution.py:24
  269.7 4.5 %collective-permute-start.24 = (f32[24,1,256]{2,1,0:T(1,128)S(1)}, f32[24,1,256]{2,1,0:T(1,128)S(1)}, u32[]{:S(2)}, u32[]{:S(2)}) collective-permute-start(f32[24,1,256]{2,1,0:T(1,128)S(1)} %get-tuple-element.142), channel_id=1, source_target_pairs={{0,1},{1,2},{2,3},{3,4},{4,5},{5,6},{6,7},{7,8},{8,9},{9,10},{10,1... | collective-permute-start | bytes 73736 | tf_op jit(solution)/shard_map/ppermute | solution.py:21
  271.6 8.5 %collective-permute-start.23 = (f32[24,1,256]{2,1,0:T(1,128)S(1)}, f32[24,1,256]{2,1,0:T(1,128)S(1)}, u32[]{:S(2)}, u32[]{:S(2)}) collective-permute-start(f32[24,1,256]{2,1,0:T(1,128)S(1)} %get-tuple-element.141), channel_id=1, source_target_pairs={{1,0},{2,1},{3,2},{4,3},{5,4},{6,5},{7,6},{8,7},{9,8},{10,9},{11,1... | collective-permute-start | bytes 73736 | tf_op jit(solution)/shard_map/ppermute | solution.py:24
  287.6 5.5 %collective-permute-start.25 = (f32[12,8,256]{2,1,0:T(8,128)S(1)}, f32[12,8,256]{2,1,0:T(8,128)S(1)}, u32[]{:S(2)}, u32[]{:S(2)}) collective-permute-start(f32[12,8,256]{2,1,0:T(8,128)S(1)} %get-tuple-element.134), channel_id=1, source_target_pairs={{64,0},{128,64},{192,128},{65,1},{129,65},{193,129},{66,2},{130,66... | collective-permute-start | bytes 294920 | tf_op jit(solution)/shard_map/ppermute | solution.py:32
  294.2 5.2 %collective-permute-start.27 = (f32[24,1,256]{2,1,0:T(1,128)S(1)}, f32[24,1,256]{2,1,0:T(1,128)S(1)}, u32[]{:S(2)}, u32[]{:S(2)}) collective-permute-start(f32[24,1,256]{2,1,0:T(1,128)S(1)} %get-tuple-element.201), channel_id=1, source_target_pairs={{0,1},{1,2},{2,3},{3,4},{4,5},{5,6},{6,7},{7,8},{8,9},{9,10},{10,1... | collective-permute-start | bytes 73736 | tf_op jit(solution)/shard_map/ppermute | solution.py:21
  297.3 8.5 %collective-permute-start.26 = (f32[24,1,256]{2,1,0:T(1,128)S(1)}, f32[24,1,256]{2,1,0:T(1,128)S(1)}, u32[]{:S(2)}, u32[]{:S(2)}) collective-permute-start(f32[24,1,256]{2,1,0:T(1,128)S(1)} %get-tuple-element.200), channel_id=1, source_target_pairs={{1,0},{2,1},{3,2},{4,3},{5,4},{6,5},{7,6},{8,7},{9,8},{10,9},{11,1... | collective-permute-start | bytes 73736 | tf_op jit(solution)/shard_map/ppermute | solution.py:24
  314.2 4.5 %collective-permute-start.29 = (f32[24,1,256]{2,1,0:T(1,128)S(1)}, f32[24,1,256]{2,1,0:T(1,128)S(1)}, u32[]{:S(2)}, u32[]{:S(2)}) collective-permute-start(f32[24,1,256]{2,1,0:T(1,128)S(1)} %get-tuple-element.193), channel_id=1, source_target_pairs={{0,1},{1,2},{2,3},{3,4},{4,5},{5,6},{6,7},{7,8},{8,9},{9,10},{10,1... | collective-permute-start | bytes 73736 | tf_op jit(solution)/shard_map/ppermute | solution.py:21
  316.2 8.5 %collective-permute-start.28 = (f32[24,1,256]{2,1,0:T(1,128)S(1)}, f32[24,1,256]{2,1,0:T(1,128)S(1)}, u32[]{:S(2)}, u32[]{:S(2)}) collective-permute-start(f32[24,1,256]{2,1,0:T(1,128)S(1)} %get-tuple-element.192), channel_id=1, source_target_pairs={{1,0},{2,1},{3,2},{4,3},{5,4},{6,5},{7,6},{8,7},{9,8},{10,9},{11,1... | collective-permute-start | bytes 73736 | tf_op jit(solution)/shard_map/ppermute | solution.py:24
  333.1 4.5 %collective-permute-start.31 = (f32[24,1,256]{2,1,0:T(1,128)S(1)}, f32[24,1,256]{2,1,0:T(1,128)S(1)}, u32[]{:S(2)}, u32[]{:S(2)}) collective-permute-start(f32[24,1,256]{2,1,0:T(1,128)S(1)} %get-tuple-element.185), channel_id=1, source_target_pairs={{0,1},{1,2},{2,3},{3,4},{4,5},{5,6},{6,7},{7,8},{8,9},{9,10},{10,1... | collective-permute-start | bytes 73736 | tf_op jit(solution)/shard_map/ppermute | solution.py:21
  335.0 8.5 %collective-permute-start.30 = (f32[24,1,256]{2,1,0:T(1,128)S(1)}, f32[24,1,256]{2,1,0:T(1,128)S(1)}, u32[]{:S(2)}, u32[]{:S(2)}) collective-permute-start(f32[24,1,256]{2,1,0:T(1,128)S(1)} %get-tuple-element.184), channel_id=1, source_target_pairs={{1,0},{2,1},{3,2},{4,3},{5,4},{6,5},{7,6},{8,7},{9,8},{10,9},{11,1... | collective-permute-start | bytes 73736 | tf_op jit(solution)/shard_map/ppermute | solution.py:24
  351.9 4.5 %collective-permute-start.33 = (f32[24,1,256]{2,1,0:T(1,128)S(1)}, f32[24,1,256]{2,1,0:T(1,128)S(1)}, u32[]{:S(2)}, u32[]{:S(2)}) collective-permute-start(f32[24,1,256]{2,1,0:T(1,128)S(1)} %get-tuple-element.177), channel_id=1, source_target_pairs={{0,1},{1,2},{2,3},{3,4},{4,5},{5,6},{6,7},{7,8},{8,9},{9,10},{10,1... | collective-permute-start | bytes 73736 | tf_op jit(solution)/shard_map/ppermute | solution.py:21
  353.8 8.5 %collective-permute-start.32 = (f32[24,1,256]{2,1,0:T(1,128)S(1)}, f32[24,1,256]{2,1,0:T(1,128)S(1)}, u32[]{:S(2)}, u32[]{:S(2)}) collective-permute-start(f32[24,1,256]{2,1,0:T(1,128)S(1)} %get-tuple-element.176), channel_id=1, source_target_pairs={{1,0},{2,1},{3,2},{4,3},{5,4},{6,5},{7,6},{8,7},{9,8},{10,9},{11,1... | collective-permute-start | bytes 73736 | tf_op jit(solution)/shard_map/ppermute | solution.py:24
  (90 other events, 182.9 us)
where the time goes:
time: 374 us; the launch traced here: 370 us
  starting transfers between devices  136 us (36%)
  local copies, waits for them, and re-layouts  105 us (28%)
  other arithmetic  78.8 us (21%)
  waiting for transfers between devices  39 us (10%)
  matrix products  7.09 us (2%)
  between operations  3.98 us (1%)
    ppermute x16, starting transfers between devices, with_halo(): lax.ppermute(lax.slice_in_dim(block, block.shape[dim] - width, None, axis...  82.1 us
    gather x16, local copies, waits for them, and re-layouts, sample(): return jnp.sum(weights * current.reshape(-1)[indices], axis=0)  50.4 us
    scatter-add x8, other arithmetic, spread(): adjoint.reshape(-1).at[indices.reshape(-1)]  49.2 us
    ppermute x16, waiting for transfers between devices, with_halo(): lax.ppermute(lax.slice_in_dim(block, 0, width, axis=dim), axis, backward)  36.4 us
    ppermute x16, starting transfers between devices, with_halo(): lax.ppermute(lax.slice_in_dim(block, 0, width, axis=dim), axis, backward)  33.4 us
    unnamed x241, local copies, waits for them, and re-layouts  28.6 us
    slice x60, local copies, waits for them, and re-layouts, across(): return 0.5 * (jnp.roll(field, -1, axis=-1) - jnp.roll(field, 1, axis=-1))  12.7 us
    all_to_all x1, starting transfers between devices, per_device(): lax.all_to_all(report_weights, 'space', split_axis=2, concat_axis=2, tile...  7.88 us
  transfers between devices with their start and end apart: 36, of which 7 were waited for; matrix products, arithmetic and copies ran while one was open for 31% of the time, Pallas kernels for 0%

commit v1 on v0

v1 whole, which is shorter than its diff:
```python
import jax
import jax.numpy as jnp
import numpy as np
from jax import lax
from jax.experimental import pallas as pl
from jax.experimental.pallas import tpu as pltpu
from jax.sharding import PartitionSpec as P

coupling = np.array(
    [[1.0, 0.55, 0.3, 0.15], [0.5, 0.9, 0.45, 0.25], [0.3, 0.4, 0.8, 0.35], [0.1, 0.2, 0.35, 0.7]],
    np.float32,
)
LEVELS = 4
VARS = 3
STEPS = 4
STRIP = 8
HALO = 4
EXT = STRIP + 2 * HALO
NX = 256
OWNERS = 64
CAP = 4
PARTS = 8
STATE_ROWS = VARS * STRIP * PARTS
FIELD_TILES = VARS * HALO
PACK = 3 * FIELD_TILES + 3

f32 = jnp.float32
bf16 = jnp.bfloat16
params = pltpu.CompilerParams(vmem_limit_bytes=48 * 2**20)


def east(z):
    return pltpu.roll(z, NX - 1, 1)


def west(z):
    return pltpu.roll(z, 1, 1)


def mix_weights(matrix):
    level = lax.broadcasted_iota(jnp.int32, (PARTS, NX), 0) % LEVELS
    weights = []
    for shift in range(1 - LEVELS, LEVELS):
        weight = jnp.zeros((PARTS, NX), f32)
        for l in range(LEVELS):
            if 0 <= l + shift < LEVELS:
                weight = jnp.where(level == l, float(matrix[l, l + shift]), weight)
        weights.append((shift, weight))
    return weights


def mix(z, weights):
    total = None
    for shift, weight in weights:
        term = weight * (z if shift == 0 else pltpu.roll(z, (-shift) % PARTS, 0))
        total = term if total is None else total + term
    return total


def split(x):
    high = x.astype(bf16)
    return high, (x - high.astype(f32)).astype(bf16)


def parity():
    return lax.axis_index("space") % 2 == 0


def state_rows(ref, v):
    return jnp.swapaxes(ref[:, v], 0, 1)


def owner_of_lane():
    lane = lax.broadcasted_iota(jnp.int32, (OWNERS, NX), 1)
    return lane // CAP == lax.broadcasted_iota(jnp.int32, (OWNERS, NX), 0)


def decode(report, k):
    p = report.astype(jnp.int32)
    channel = p >> 11
    level = (channel * 11) >> 5
    variable = channel - 3 * level
    code = (variable * STRIP + ((p >> 8) & 7)) * PARTS + level
    code = jnp.where(p < 0, -1024, code)
    return code + k * LEVELS, p & (NX - 1)


def one_hot_columns(column):
    place = lax.broadcasted_iota(jnp.int32, (NX, NX), 0)
    return jnp.where(place == column, 1.0, 0.0).astype(f32).astype(bf16)


def pack_kernel(inc, bg, mult, cells, offsets, counts, out_a, out_b, rep):
    even = parity()
    for f, ref in enumerate((inc, bg, mult)):
        for v in range(VARS):
            rows = state_rows(ref, v)
            low, high = rows[:HALO], rows[STRIP - HALO :]
            at = f * FIELD_TILES + v * HALO
            out_a[at : at + HALO] = jnp.where(even, high, low)
            out_b[at : at + HALO] = jnp.where(even, low, high)
    slot = lax.broadcasted_iota(jnp.int32, (PARTS, NX), 1) % CAP
    count = jnp.concatenate([counts[0], counts[1]], axis=0).astype(f32).astype(bf16)
    spread = jnp.where(owner_of_lane(), 1.0, 0.0).astype(f32).astype(bf16)
    live = slot.astype(f32) < jnp.dot(count, spread, preferred_element_type=f32)
    cell = jnp.concatenate([cells[0], cells[1]], axis=0).astype(f32)
    rep[0] = jnp.where(live, cell, -1.0)
    for k in range(2):
        for j in range(STEPS):
            for side in range(2):
                rep[1 + side, pl.ds(k * STEPS + j, 1), :] = offsets[k, j, pl.ds(side, 1), :]
    for n in range(3):
        out_a[3 * FIELD_TILES + n] = rep[n]
        out_b[3 * FIELD_TILES + n] = rep[n]


def tangent_kernel(
    inc, bg, mult, rep, got_a, got_b, owned, final0, final1, outer, send, state, back, raised, vals
):
    s = lax.axis_index("space")
    even = s % 2 == 0
    top = jnp.where(s > 0, 1.0, 0.0).astype(f32)
    bottom = jnp.where(s < OWNERS - 1, 1.0, 0.0).astype(f32)

    def halo_rows(f, v, i):
        at = f * FIELD_TILES + v * HALO + i
        a, b = got_a[at], got_b[at]
        return jnp.where(even, b, a), jnp.where(even, a, b)

    for v in range(VARS):
        for i in range(HALO):
            low, high = halo_rows(0, v, i)
            state[0, v, i] = low
            state[0, v, HALO + STRIP + i] = high
            low, high = halo_rows(1, v, i)
            back[v, i] = low
            back[v, HALO + STRIP + i] = high
        state[0, v, HALO : HALO + STRIP] = state_rows(inc, v)
        back[v, HALO : HALO + STRIP] = state_rows(bg, v)

    first = lax.broadcasted_iota(jnp.int32, (PARTS, NX), 0) < LEVELS
    for v in range(VARS):
        lows, highs = [], []
        for i in range(HALO):
            low, high = halo_rows(2, v, i)
            lows.append(low)
            highs.append(high)
        middle = state_rows(mult, v)
        rows = lows + [middle[r] for r in range(STRIP)] + highs
        for i in range(EXT // 2):
            outer[v * (EXT // 2) + i] = jnp.where(
                first, rows[i], pltpu.roll(rows[i + EXT // 2], LEVELS, 0)
            )

    weights = mix_weights(coupling)
    part = lax.broadcasted_iota(jnp.int32, (PARTS, NX), 0)
    cells = rep[0]
    for j in range(STEPS):
        now, later = j % 2, (j + 1) % 2
        x = jnp.concatenate(
            [state[now, v, HALO : HALO + STRIP].reshape(STRIP * PARTS, NX) for v in range(VARS)],
            axis=0,
        )
        high, low = split(x)
        high_e, low_e = split(east(x))
        stacked = jnp.concatenate([high, low, high_e, low_e], axis=0)
        for k in range(2):
            n = k * STEPS + j
            code, column = decode(cells[n : n + 1], k)
            picked = jnp.dot(stacked, one_hot_columns(column), preferred_element_type=f32)
            sums = [jnp.zeros((PARTS, NX), f32) for _ in range(4)]
            for v in range(VARS):
                before = None
                for r in range(STRIP):
                    at = (v * STRIP + r) * PARTS
                    here = code == part + at
                    t0 = picked[at : at + PARTS] + picked[STATE_ROWS + at : STATE_ROWS + at + PARTS]
                    t1 = (
                        picked[2 * STATE_ROWS + at : 2 * STATE_ROWS + at + PARTS]
                        + picked[3 * STATE_ROWS + at : 3 * STATE_ROWS + at + PARTS]
                    )
                    sums[0] = jnp.where(here, t0, sums[0])
                    sums[1] = jnp.where(here, t1, sums[1])
                    if before is not None:
                        sums[2] = jnp.where(before, t0, sums[2])
                        sums[3] = jnp.where(before, t1, sums[3])
                    before = here
            a, b = rep[1, n : n + 1], rep[2, n : n + 1]
            value = (1.0 - b) * ((1.0 - a) * sums[0] + a * sums[1]) + b * (
                (1.0 - a) * sums[2] + a * sums[3]
            )
            vals[pl.ds(n, 1), :] = jnp.sum(value, axis=0, keepdims=True)
        for row in range(j, EXT - j):
            raised[row] = mix(state[now, 2, row], weights)
        for row in range(j + 1, EXT - 1 - j):
            ub, vb, hb = back[0, row], back[1, row], back[2, row]
            centre = [state[now, v, row] for v in range(VARS)]
            up = [state[now, v, row + 1] for v in range(VARS)]
            down = [state[now, v, row - 1] for v in range(VARS)]
            e = [east(z) for z in centre]
            w = [west(z) for z in centre]
            cols = [e[v] - w[v] for v in range(VARS)]
            rows = [up[v] - down[v] for v in range(VARS)]
            smooth = [up[v] + down[v] + (e[v] + w[v]) for v in range(VARS)]
            lift = raised[row]
            push_c = east(lift) - west(lift)
            push_r = raised[row + 1] - raised[row - 1]
            ub, vb, hb = 0.05 * ub, 0.05 * vb, 0.05 * hb
            new = [
                0.98 * centre[0]
                + 0.03 * centre[1]
                + 0.005 * smooth[0]
                - 0.05 * push_c
                - (ub * cols[0] + vb * rows[0]),
                0.98 * centre[1]
                - 0.03 * centre[0]
                + 0.005 * smooth[1]
                - 0.05 * push_r
                - (ub * cols[1] + vb * rows[1]),
                0.98 * centre[2]
                + 0.005 * smooth[2]
                - hb * (cols[0] + rows[1])
                - (ub * cols[2] + vb * rows[2]),
            ]
            for v in range(VARS):
                value = new[v]
                if row < HALO:
                    value = value * top
                elif row >= HALO + STRIP:
                    value = value * bottom
                state[later, v, row] = value
    last = STEPS % 2
    for v in range(VARS):
        value = jnp.swapaxes(state[last, v, HALO : HALO + STRIP], 0, 1)
        final0[:, v] = value[:LEVELS]
        final1[:, v] = value[LEVELS:]
    own = jnp.concatenate([owned[0], owned[1]], axis=0)
    slot = lax.broadcasted_iota(jnp.int32, (PARTS, NX), 1) % CAP
    pieces = []
    for piece in (pltpu.roll(own, CAP, 1), own, pltpu.roll(own, NX - CAP, 1), vals[...]):
        for i in range(CAP):
            pieces.append(jnp.where(slot == i, piece, 0.0))
    chosen = jnp.where(owner_of_lane(), 1.0, 0.0).astype(f32)
    send[...] = lax.dot_general(
        chosen,
        jnp.concatenate(pieces, axis=0),
        (((1,), (1,)), ((), ())),
        precision=lax.Precision.HIGHEST,
        preferred_element_type=f32,
    )


def adjoint_kernel(
    mult,
    bg,
    variance,
    inc,
    rep,
    got_a,
    got_b,
    outer,
    final0,
    incoming,
    got,
    owned,
    owned_variance,
    model_out,
    report_out,
    image_out,
    state,
    back,
    flux,
):
    s = lax.axis_index("space")
    even = s % 2 == 0
    top = jnp.where(s > 0, 1.0, 0.0).astype(f32)
    bottom = jnp.where(s < OWNERS - 1, 1.0, 0.0).astype(f32)
    for part, before in ((slice(0, LEVELS), incoming), (slice(LEVELS, PARTS), final0)):
        model_out[part] = variance[part] * mult[part] + inc[part] - before[...]

    chosen = jnp.where(owner_of_lane(), 1.0, 0.0).astype(f32)
    spread = lax.dot_general(
        jnp.transpose(got[...]),
        chosen,
        (((1,), (0,)), ((), ())),
        precision=lax.Precision.HIGHEST,
        preferred_element_type=f32,
    )
    slot = lax.broadcasted_iota(jnp.int32, (PARTS, NX), 1) % CAP
    loads = []
    for g in range(4):
        value = jnp.zeros((PARTS, NX), f32)
        for i in range(CAP):
            at = (g * CAP + i) * PARTS
            value = jnp.where(slot == i, spread[at : at + PARTS], value)
        loads.append(value)
    for k in range(2):
        report_out[k] = (
            owned_variance[k] * owned[k] + loads[3][k * STEPS : (k + 1) * STEPS]
        )

    def halo_rows(f, v, i):
        at = f * FIELD_TILES + v * HALO + i
        a, b = got_a[at], got_b[at]
        return jnp.where(even, b, a), jnp.where(even, a, b)

    first = lax.broadcasted_iota(jnp.int32, (PARTS, NX), 0) < LEVELS
    for v in range(VARS):
        lows, highs = [], []
        for i in range(HALO):
            low, high = halo_rows(1, v, i)
            back[v, i] = low
            back[v, HALO + STRIP + i] = high
            low, high = halo_rows(2, v, i)
            lows.append(low)
            highs.append(high)
        back[v, HALO : HALO + STRIP] = state_rows(bg, v)
        middle = state_rows(mult, v)
        rows = lows + [middle[r] for r in range(STRIP)] + highs
        for i in range(EXT):
            after = outer[v * (EXT // 2) + i % (EXT // 2)]
            if i < EXT // 2:
                after = pltpu.roll(after, LEVELS, 0)
            state[0, v, i] = -jnp.where(first, pltpu.roll(rows[i], LEVELS, 0), after)

    reports = []
    base = 3 * FIELD_TILES
    for n in range(3):
        a, b = got_a[base + n], got_b[base + n]
        reports.append((jnp.where(even, b, a), rep[n], jnp.where(even, a, b)))
    part = lax.broadcasted_iota(jnp.int32, (PARTS, NX), 0)

    def field(side, j, rows):
        lhs, rhs = [], []
        for k in range(2):
            n = k * STEPS + j
            code, column = decode(reports[0][side][n : n + 1], k)
            a, b = reports[1][side][n : n + 1], reports[2][side][n : n + 1]
            load = loads[side][n : n + 1]
            parts = []
            for share in ((1.0 - a) * load, a * load):
                own, following = (1.0 - b) * share, b * share
                tiles = []
                for v in range(VARS):
                    for r in rows:
                        at = (v * STRIP + r) * PARTS
                        tile = jnp.where(code == part + at, own, 0.0)
                        if r > 0:
                            tile = jnp.where(code == part + (at - PARTS), following, tile)
                        tiles.append(tile)
                parts += list(split(jnp.concatenate(tiles, axis=0)))
            lhs.append(jnp.concatenate(parts, axis=0))
            rhs.append(one_hot_columns(column))
        out = lax.dot_general(
            jnp.concatenate(lhs, axis=1),
            jnp.concatenate(rhs, axis=1),
            (((1,), (1,)), ((), ())),
            preferred_element_type=f32,
        )
        count = VARS * len(rows) * PARTS
        total = out[:count] + out[count : 2 * count]
        total = total + west(out[2 * count : 3 * count] + out[3 * count :])
        tiles = {}
        for v in range(VARS):
            for at, r in enumerate(rows):
                first_row = (v * len(rows) + at) * PARTS
                tiles[v, r] = total[first_row : first_row + PARTS]
        return tiles

    weights = mix_weights(coupling.T)
    for step, j in enumerate(reversed(range(STEPS))):
        now, later = step % 2, (step + 1) % 2
        added = {}
        for (v, r), tile in field(1, j, list(range(STRIP))).items():
            added[v, HALO + r] = tile
        if j > 0:
            for (v, r), tile in field(0, j, list(range(STRIP - j, STRIP))).items():
                added[v, HALO + r - STRIP] = tile
            for (v, r), tile in field(2, j, list(range(j))).items():
                added[v, HALO + r + STRIP] = tile
        for row in range(step, EXT - step):
            ub, vb, hb = back[0, row], back[1, row], back[2, row]
            au, av, ah = state[now, 0, row], state[now, 1, row], state[now, 2, row]
            flux[0, row] = vb * au
            flux[1, row] = hb * ah + vb * av
            flux[2, row] = vb * ah + mix(av, weights)
        for row in range(step + 1, EXT - 1 - step):
            ub, vb, hb = back[0, row], back[1, row], back[2, row]
            centre = [state[now, v, row] for v in range(VARS)]
            au, av, ah = centre
            across = [hb * ah + ub * au, ub * av, ub * ah + mix(au, weights)]
            turn = [0.98 * au - 0.03 * av, 0.98 * av + 0.03 * au, 0.98 * ah]
            for v in range(VARS):
                near = (
                    state[now, v, row + 1]
                    + state[now, v, row - 1]
                    + (east(centre[v]) + west(centre[v]))
                )
                value = (
                    turn[v]
                    + 0.005 * near
                    + 0.05
                    * (
                        (east(across[v]) - west(across[v]))
                        + (flux[v, row + 1] - flux[v, row - 1])
                    )
                    + added[v, row]
                )
                if row < HALO:
                    value = value * top
                elif row >= HALO + STRIP:
                    value = value * bottom
                state[later, v, row] = value
    last = STEPS % 2
    for v in range(VARS):
        value = jnp.swapaxes(state[last, v, HALO : HALO + STRIP], 0, 1)
        image_out[:, v] = mult[:, v] + value


def vmem(count):
    return [pl.BlockSpec(memory_space=pltpu.VMEM)] * count


def shaped(*shape):
    return jax.ShapeDtypeStruct(shape, f32)


def per_device(
    multipliers,
    increments,
    background,
    error_variance,
    report_weights,
    report_variance,
    report_cells,
    report_offsets,
    report_counts,
):
    mult, inc, bg, variance = (
        x.reshape(PARTS, VARS, STRIP, NX) for x in (multipliers, increments, background, error_variance)
    )
    count = lax.axis_size("space")
    wins = lax.axis_size("win")
    pack_a, pack_b, rep = pl.pallas_call(
        pack_kernel,
        name="pack",
        out_shape=(shaped(PACK, PARTS, NX), shaped(PACK, PARTS, NX), shaped(3, PARTS, NX)),
        in_specs=vmem(6),
        out_specs=vmem(3),
        compiler_params=params,
    )(inc, bg, mult, report_cells, report_offsets, report_counts)
    inner = [(i, i + 1) for i in range(0, count, 2)]
    outward = [(i, i + 1) for i in range(1, count - 1, 2)]
    both = lambda pairs: pairs + [(target, source) for source, target in pairs]
    got_b = lax.ppermute(pack_b, "space", both(outward))
    got_a = lax.ppermute(pack_a, "space", both(inner))
    final0, final1, outer, send = pl.pallas_call(
        tangent_kernel,
        name="tangent",
        out_shape=(
            shaped(LEVELS, VARS, STRIP, NX),
            shaped(LEVELS, VARS, STRIP, NX),
            shaped(VARS * EXT // 2, PARTS, NX),
            shaped(OWNERS, 4 * CAP * PARTS),
        ),
        in_specs=vmem(7),
        out_specs=vmem(4),
        scratch_shapes=[
            pltpu.VMEM((2, VARS, EXT, PARTS, NX), f32),
            pltpu.VMEM((VARS, EXT, PARTS, NX), f32),
            pltpu.VMEM((EXT, PARTS, NX), f32),
            pltpu.VMEM((PARTS, NX), f32),
        ],
        compiler_params=params,
    )(inc, bg, mult, rep, got_a, got_b, report_weights)
    outer = lax.ppermute(outer, "win", [(i + 1, i) for i in range(wins - 1)])
    got = lax.all_to_all(send, "space", split_axis=0, concat_axis=0, tiled=True)
    incoming = lax.ppermute(final1, "win", [(i, i + 1) for i in range(wins - 1)])
    model, report, image = pl.pallas_call(
        adjoint_kernel,
        name="adjoint",
        out_shape=(
            shaped(PARTS, VARS, STRIP, NX),
            shaped(2, STEPS, NX),
            shaped(PARTS, VARS, STRIP, NX),
        ),
        in_specs=vmem(13),
        out_specs=vmem(3),
        scratch_shapes=[
            pltpu.VMEM((2, VARS, EXT, PARTS, NX), f32),
            pltpu.VMEM((VARS, EXT, PARTS, NX), f32),
            pltpu.VMEM((VARS, EXT, PARTS, NX), f32),
        ],
        compiler_params=params,
    )(
        mult,
        bg,
        variance,
        inc,
        rep,
        got_a,
        got_b,
        outer,
        final0,
        incoming,
        got,
        report_weights,
        report_variance,
    )
    return model.reshape(multipliers.shape), report, image.reshape(multipliers.shape)


def solution(mesh):
    state = P("win", None, "space", None)
    slots = P("win", None, "space")
    return jax.shard_map(
        per_device,
        mesh=mesh,
        in_specs=(state, state, state, state, slots, slots, slots, P("win", None, None, "space"), slots),
        out_specs=(state, slots, state),
        check_vma=False,
    )
```

time: 374 us -> 50.4 us (0.13)
  the two profiles are of different devices: /device:TPU:111 before, /device:TPU:1 now
where the time goes in v1:
time: 50.4 us; the launch traced here: 50 us
  blocking collectives  20.9 us (41%)
  starting transfers between devices  10.4 us (21%)
  Pallas kernels  6.7 us (13%)
  waiting for transfers between devices  6.37 us (13%)
  local copies, waits for them, and re-layouts  4.89 us (10%)
  between operations  0.7 us (1%)
    all_to_all x1, blocking collectives, per_device(): got = lax.all_to_all(send, 'space', split_axis=0, concat_axis=0, tiled=True)  20.9 us
    ppermute x1, waiting for transfers between devices, per_device(): got_b = lax.ppermute(pack_b, 'space', both(outward))  6.37 us
    unnamed x18, local copies, waits for them, and re-layouts  4.89 us
    pallas_call x1, Pallas kernels, per_device(): pl.pallas_call(adjoint_kernel, name='adjoint', out_shape=(shaped(PARTS, V...  4.13 us
    ppermute x1, starting transfers between devices, per_device(): lax.ppermute(final1, 'win', [(i, i + 1) for i in range(wins - 1)])  3.99 us
    ppermute x1, starting transfers between devices, per_device(): got_a = lax.ppermute(pack_a, 'space', both(inner))  3.24 us
    pallas_call x1, Pallas kernels, per_device(): pl.pallas_call(tangent_kernel, name='tangent', out_shape=(shaped(LEVELS,...  2.32 us
    ppermute x1, starting transfers between devices, per_device(): got_b = lax.ppermute(pack_b, 'space', both(outward))  1.91 us
  transfers between devices with their start and end apart: 4, of which 1 were waited for; matrix products, arithmetic and copies ran while one was open for 0% of the time, Pallas kernels for 0%

profile of v1, /device:TPU:1, one launch (start us, length us, event | category | flops | bytes accessed | tf_op | source)
XLA Modules:
  0.0 50.0 jit_solution(6074483236474215021)
XLA Ops:
  0.6 0.0 copy-start.8
  0.6 0.7 %copy-done.8 = s32[2,4,64]{2,1,0:T(4,128)S(1)} copy-done((s32[2,4,64]{2,1,0:T(4,128)S(1)}, s32[2,4,64]{2,1,0:T(4,128)}, u32[]{:S(2)}) %copy-start.8) | copy-done | bytes 2072
  1.3 0.0 copy-start
  1.3 0.9 %copy-done = f32[2,12,8,256]{3,2,1,0:T(8,128)S(1)} copy-done((f32[2,12,8,256]{3,2,1,0:T(8,128)S(1)}, f32[2,12,8,256]{3,2,1,0:T(8,128)}, u32[]{:S(2)}) %copy-start) | copy-done | bytes 196632
  2.2 0.0 copy-start.1
  2.2 0.9 %copy-done.1 = f32[2,12,8,256]{3,2,1,0:T(8,128)S(1)} copy-done((f32[2,12,8,256]{3,2,1,0:T(8,128)S(1)}, f32[2,12,8,256]{3,2,1,0:T(8,128)}, u32[]{:S(2)}) %copy-start.1) | copy-done | bytes 196632
  3.2 0.0 copy-start.2
  3.2 0.9 %copy-done.2 = f32[2,12,8,256]{3,2,1,0:T(8,128)S(1)} copy-done((f32[2,12,8,256]{3,2,1,0:T(8,128)S(1)}, f32[2,12,8,256]{3,2,1,0:T(8,128)}, u32[]{:S(2)}) %copy-start.2) | copy-done | bytes 196632
  4.1 0.0 copy-start.5
  4.1 0.7 %copy-done.5 = f32[2,4,2,256]{3,2,1,0:T(2,128)S(1)} copy-done((f32[2,4,2,256]{3,2,1,0:T(2,128)S(1)}, f32[2,4,2,256]{3,2,1,0:T(2,128)}, u32[]{:S(2)}) %copy-start.5) | copy-done | bytes 16408
  4.8 0.0 copy-start.6
  4.8 0.7 %copy-done.6 = s32[2,4,256]{2,1,0:T(4,128)S(1)} copy-done((s32[2,4,256]{2,1,0:T(4,128)S(1)}, s32[2,4,256]{2,1,0:T(4,128)}, u32[]{:S(2)}) %copy-start.6) | copy-done | bytes 8216
  5.5 0.0 copy-start.4
  5.5 0.2 pack.1
  5.8 3.2 %collective-permute-start = (f32[39,8,256]{2,1,0:T(8,128)S(1)}, f32[39,8,256]{2,1,0:T(8,128)S(1)}, u32[]{:S(2)}, u32[]{:S(2)}) collective-permute-start(f32[39,8,256]{2,1,0:T(8,128)S(1)} %get-tuple-element.14), channel_id=1, source_target_pairs={{0,1},{2,3},{4,5},{6,7},{8,9},{10,11},{12,13},{14,15},{16,17},{18,... | collective-permute-start | bytes 958472 | tf_op jit(solution)/shard_map/ppermute | solution.py:456
  9.0 1.9 %collective-permute-start.1 = (f32[39,8,256]{2,1,0:T(8,128)S(1)}, f32[39,8,256]{2,1,0:T(8,128)S(1)}, u32[]{:S(2)}, u32[]{:S(2)}) collective-permute-start(f32[39,8,256]{2,1,0:T(8,128)S(1)} %get-tuple-element.15), channel_id=1, source_target_pairs={{1,2},{3,4},{5,6},{7,8},{9,10},{11,12},{13,14},{15,16},{17,18},{19... | collective-permute-start | bytes 958472 | tf_op jit(solution)/shard_map/ppermute | solution.py:455
  10.9 0.0 collective-permute-done.got_a
  10.9 6.4 %collective-permute-done.1.got_b = f32[39,8,256]{2,1,0:T(8,128)S(1)} collective-permute-done((f32[39,8,256]{2,1,0:T(8,128)S(1)}, f32[39,8,256]{2,1,0:T(8,128)S(1)}, u32[]{:S(2)}, u32[]{:S(2)}) %collective-permute-start.1) | collective-permute-done | bytes 319520 | tf_op jit(solution)/shard_map/ppermute | solution.py:455
  17.3 0.0 copy-done.4
  17.3 0.0 copy-start.3
  17.3 2.3 %tangent.1 = (f32[4,3,8,256]{3,2,1,0:T(8,128)S(1)}, f32[4,3,8,256]{3,2,1,0:T(8,128)S(1)}, f32[24,8,256]{2,1,0:T(8,128)S(1)}, f32[64,128]{1,0:T(8,128)S(1)}) custom-call(f32[8,3,8,256]{3,2,1,0:T(8,128)S(1)} %bitcast.17, f32[8,3,8,256]{3,2,1,0:T(8,128)S(1)} %bitcast.14, f32[8,3,8,256]{3,2,1,0:T(8,128)S(1)} %bitcast.11, ...), custom_call_target="tpu_custom_call" | custom-call | tf_op jit(solution)/shard_map/tangent/pallas_call | solution.py:457
  19.6 1.3 %collective-permute-start.2 = (f32[24,8,256]{2,1,0:T(8,128)S(1)}, f32[24,8,256]{2,1,0:T(8,128)S(1)}, u32[]{:S(2)}, u32[]{:S(2)}) collective-permute-start(f32[24,8,256]{2,1,0:T(8,128)S(1)} %get-tuple-element.16), channel_id=1, source_target_pairs={{64,0},{128,64},{192,128},{65,1},{129,65},{193,129},{66,2},{130,66... | collective-permute-start | bytes 589832 | tf_op jit(solution)/shard_map/ppermute | solution.py:476
  20.9 4.0 %collective-permute-start.3 = (f32[4,3,8,256]{3,2,1,0:T(8,128)S(1)}, f32[4,3,8,256]{3,2,1,0:T(8,128)S(1)}, u32[]{:S(2)}, u32[]{:S(2)}) collective-permute-start(f32[4,3,8,256]{3,2,1,0:T(8,128)S(1)} %get-tuple-element.18), channel_id=1, source_target_pairs={{0,64},{64,128},{128,192},{1,65},{65,129},{129,193},{2,66},{66,130... | collective-permute-start | bytes 294920 | tf_op jit(solution)/shard_map/ppermute | solution.py:478
  24.9 0.0 copy-start.7
  25.0 20.9 %all_to_all.11 = f32[64,1,128]{2,1,0:T(1,128)S(1)} all-to-all(f32[64,1,128]{2,1,0:T(1,128)S(1)} %bitcast.21), channel_id=1, replica_groups=mesh['win'=4,'space'=64] {'space'}, dimensions={0} | all-to-all | bytes 65536 | tf_op jit(solution)/shard_map/all_to_all | solution.py:477
  45.8 0.0 collective-permute-done.3.incoming
  45.8 0.0 collective-permute-done.2.outer
  45.8 0.0 copy-done.3
  45.8 0.0 copy-done.7
  45.9 4.1 %adjoint.1 = (f32[8,3,8,256]{3,2,1,0:T(8,128)}, f32[2,4,256]{2,1,0:T(4,128)}, f32[8,3,8,256]{3,2,1,0:T(8,128)}) custom-call(f32[8,3,8,256]{3,2,1,0:T(8,128)S(1)} %bitcast.12, f32[8,3,8,256]{3,2,1,0:T(8,128)S(1)} %bitcast.15, f32[8,3,8,256]{3,2,1,0:T(8,128)S(1)} %bitcast.19, f32[8,3,8,256]{3,2,1,0:T(8,128)S(1)} %bitcast.18, ...), custom_call_target="tpu_custom_call" | custom-call | tf_op jit(solution)/shard_map/adjoint/pallas_call | solution.py:479
Async XLA Ops:
  0.6 0.7 %copy-start.8 = (s32[2,4,64]{2,1,0:T(4,128)S(1)}, s32[2,4,64]{2,1,0:T(4,128)}, u32[]{:S(2)}) copy-start(s32[2,4,64]{2,1,0:T(4,128)} %counts.1) | copy-start | bytes 6148
  1.3 0.9 %copy-start = (f32[2,12,8,256]{3,2,1,0:T(8,128)S(1)}, f32[2,12,8,256]{3,2,1,0:T(8,128)}, u32[]{:S(2)}) copy-start(f32[2,12,8,256]{3,2,1,0:T(8,128)} %param.9) | copy-start | bytes 589828
  2.2 0.9 %copy-start.1 = (f32[2,12,8,256]{3,2,1,0:T(8,128)S(1)}, f32[2,12,8,256]{3,2,1,0:T(8,128)}, u32[]{:S(2)}) copy-start(f32[2,12,8,256]{3,2,1,0:T(8,128)} %param.11) | copy-start | bytes 589828
  3.2 0.9 %copy-start.2 = (f32[2,12,8,256]{3,2,1,0:T(8,128)S(1)}, f32[2,12,8,256]{3,2,1,0:T(8,128)}, u32[]{:S(2)}) copy-start(f32[2,12,8,256]{3,2,1,0:T(8,128)} %param.10) | copy-start | bytes 589828
  4.1 0.7 %copy-start.5 = (f32[2,4,2,256]{3,2,1,0:T(2,128)S(1)}, f32[2,4,2,256]{3,2,1,0:T(2,128)}, u32[]{:S(2)}) copy-start(f32[2,4,2,256]{3,2,1,0:T(2,128)} %offsets.1) | copy-start | bytes 49156
  4.8 0.7 %copy-start.6 = (s32[2,4,256]{2,1,0:T(4,128)S(1)}, s32[2,4,256]{2,1,0:T(4,128)}, u32[]{:S(2)}) copy-start(s32[2,4,256]{2,1,0:T(4,128)} %cells.1) | copy-start | bytes 24580
  5.5 11.8 %copy-start.4 = (f32[2,4,256]{2,1,0:T(4,128)S(1)}, f32[2,4,256]{2,1,0:T(4,128)}, u32[]{:S(2)}) copy-start(f32[2,4,256]{2,1,0:T(4,128)} %owned.3) | copy-start | bytes 24580
  5.8 5.2 %collective-permute-start = (f32[39,8,256]{2,1,0:T(8,128)S(1)}, f32[39,8,256]{2,1,0:T(8,128)S(1)}, u32[]{:S(2)}, u32[]{:S(2)}) collective-permute-start(f32[39,8,256]{2,1,0:T(8,128)S(1)} %get-tuple-element.14), channel_id=1, source_target_pairs={{0,1},{2,3},{4,5},{6,7},{8,9},{10,11},{12,13},{14,15},{16,17},{18,... | collective-permute-start | bytes 958472 | tf_op jit(solution)/shard_map/ppermute | solution.py:456
  9.0 8.3 %collective-permute-start.1 = (f32[39,8,256]{2,1,0:T(8,128)S(1)}, f32[39,8,256]{2,1,0:T(8,128)S(1)}, u32[]{:S(2)}, u32[]{:S(2)}) collective-permute-start(f32[39,8,256]{2,1,0:T(8,128)S(1)} %get-tuple-element.15), channel_id=1, source_target_pairs={{1,2},{3,4},{5,6},{7,8},{9,10},{11,12},{13,14},{15,16},{17,18},{19... | collective-permute-start | bytes 958472 | tf_op jit(solution)/shard_map/ppermute | solution.py:455
  17.3 28.5 %copy-start.3 = (f32[2,12,8,256]{3,2,1,0:T(8,128)S(1)}, f32[2,12,8,256]{3,2,1,0:T(8,128)}, u32[]{:S(2)}) copy-start(f32[2,12,8,256]{3,2,1,0:T(8,128)} %param.12) | copy-start | bytes 589828
  19.6 26.2 %collective-permute-start.2 = (f32[24,8,256]{2,1,0:T(8,128)S(1)}, f32[24,8,256]{2,1,0:T(8,128)S(1)}, u32[]{:S(2)}, u32[]{:S(2)}) collective-permute-start(f32[24,8,256]{2,1,0:T(8,128)S(1)} %get-tuple-element.16), channel_id=1, source_target_pairs={{64,0},{128,64},{192,128},{65,1},{129,65},{193,129},{66,2},{130,66... | collective-permute-start | bytes 589832 | tf_op jit(solution)/shard_map/ppermute | solution.py:476
  20.9 24.9 %collective-permute-start.3 = (f32[4,3,8,256]{3,2,1,0:T(8,128)S(1)}, f32[4,3,8,256]{3,2,1,0:T(8,128)S(1)}, u32[]{:S(2)}, u32[]{:S(2)}) collective-permute-start(f32[4,3,8,256]{3,2,1,0:T(8,128)S(1)} %get-tuple-element.18), channel_id=1, source_target_pairs={{0,64},{64,128},{128,192},{1,65},{65,129},{129,193},{2,66},{66,130... | collective-permute-start | bytes 294920 | tf_op jit(solution)/shard_map/ppermute | solution.py:478
  24.9 20.9 %copy-start.7 = (f32[2,4,256]{2,1,0:T(4,128)S(1)}, f32[2,4,256]{2,1,0:T(4,128)}, u32[]{:S(2)}) copy-start(f32[2,4,256]{2,1,0:T(4,128)} %owned_variance.1) | copy-start | bytes 24580
